TPU v7x, 128 devices: a whole 4x4x4 slice. The times are simulated.
128 devices in a mesh: grp: 2 (over core), ctx: 64 (over y, z, x).
Axes of the slice: x: 4, y: 4, z: 4, core: 2. Of those that a mesh axis runs over, the one named last changes fastest.
Arguments:
- gla_query: bfloat16 [16384, 4096], P(('grp', 'ctx')), parts along dimension 0, may hold values from -6 to 6
- gla_key: bfloat16 [16384, 4096], P(('grp', 'ctx')), parts along dimension 0, may hold values from -6 to 6
- gla_value: bfloat16 [16384, 4096], P(('grp', 'ctx')), parts along dimension 0, may hold values from -6 to 6
- log_gates: float32 [16384, 32], P(('grp', 'ctx')), parts along dimension 0, may hold values from -1.2 to 0
- norm_gain: float32 [4096], replicated, may hold values from 0.5 to 1.5
- attn_query: bfloat16 [16384, 4096], P(('grp', 'ctx')), parts along dimension 0, may hold values from -6 to 6
- attn_key: bfloat16 [16384, 4096], P(('grp', 'ctx')), parts along dimension 0, may hold values from -4 to 4
- doc_blocks: int32 [16], P('grp'), parts along dimension 0, may hold values from 1 to 32, 64 in all
Outputs:
- gla_mixed: bfloat16 [16384, 4096], P(('grp', 'ctx')), parts along dimension 0
- attended: bfloat16 [16384, 4096], P(('grp', 'ctx')), parts along dimension 0
There are 2 independent parts, one for each index of `grp`. A program takes and returns all parts, laid end to end along the dimension named above; an argument that names none is the same for every part. Nothing has to cross between parts.
Inputs may be any that keep to these rules, and one draw needn't show every extreme that they name: `doc_blocks`: the documents of a group in order, together covering all 8192 tokens; the longest has exactly 32 blocks.
All inputs are finite; a program needn't handle non-finite values.
Results may differ from a plain program's by a relative error of at most 0.0057.
Values may be sent and summed in bfloat16 or wider, within the bound.
A program may use at most 320 MiB of HBM per device.

v0:
```python
import jax
import jax.numpy as jnp
from jax import lax
from jax.sharding import PartitionSpec as P

BLOCK = 128
WINDOW = 2048


def entering_2(part, axis, combine, identity):
    place = lax.axis_index(axis)
    gathered = jax.tree.map(lambda a: lax.all_gather(a, axis), part)
    state = jax.tree.map(lambda a, e: jnp.zeros_like(a) + jnp.asarray(e, a.dtype), part, identity)

    def one(turn, state):
        return combine(
            state, jax.tree.map(lambda a: lax.dynamic_index_in_dim(a, turn, 0, False), gathered)
        )

    return lax.fori_loop(0, place, one, state)


def compose(earlier, later):
    return (earlier[0] * later[0], later[0][:, None, None] * earlier[1] + later[1])


def gla_layer(gla_query, gla_key, gla_value, log_gates, norm_gain, doc_blocks):
    tok_rows, columns = gla_query.shape
    head_count = log_gates.shape[1]
    head_dim = columns // head_count
    block_count = tok_rows // BLOCK
    offset = lax.axis_index("ctx") * tok_rows
    doc_ends = jnp.cumsum(doc_blocks) * BLOCK
    starts = doc_ends - doc_blocks * BLOCK
    block_offsets = offset + jnp.arange(block_count, dtype=jnp.int32) * BLOCK
    resets = jnp.any(block_offsets[:, None] == starts[None, :], axis=1).astype(jnp.float32)
    shaped = (block_count, BLOCK, head_count, head_dim)
    query_rows = gla_query.reshape(shaped)
    key_rows = gla_key.reshape(shaped)
    float_query = query_rows.astype(jnp.float32) * head_dim ** (-0.5)
    float_key = key_rows.astype(jnp.float32)
    float_value = gla_value.reshape(shaped).astype(jnp.float32)
    gate_sums = jnp.cumsum(log_gates.reshape(block_count, BLOCK, head_count), axis=1)
    block_last = gate_sums[:, -1, :]
    by_head = gate_sums.transpose(0, 2, 1)
    causal = (jnp.arange(BLOCK)[:, None] >= jnp.arange(BLOCK)[None, :])[None, None]
    gaps = by_head[:, :, :, None] - by_head[:, :, None, :]
    weight = jnp.where(causal, jnp.exp(jnp.where(causal, gaps, 0.0)), 0.0)
    raw_scores = jnp.einsum(
        "cthd,cshd->chts", query_rows, key_rows, preferred_element_type=jnp.float32
    )
    scores = raw_scores * head_dim ** (-0.5) * weight
    inner_part = jnp.einsum("chts,cshd->cthd", scores, float_value, precision=lax.Precision.HIGHEST)
    tails = jnp.exp(block_last[:, None, :] - gate_sums)
    local_state = jnp.einsum(
        "cshd,cshe->chde",
        float_key * tails[..., None],
        float_value,
        precision=lax.Precision.HIGHEST,
    )
    decays = jnp.exp(block_last) * (1.0 - resets)[:, None]
    total_decay = jnp.ones((head_count,), jnp.float32)
    total_state = jnp.zeros((head_count, head_dim, head_dim), jnp.float32)
    block_id = 0
    total_decay, total_state = compose(
        (total_decay, total_state), (decays[block_id], local_state[block_id])
    )
    identity = (
        jnp.ones((head_count,), jnp.float32),
        jnp.zeros((head_count, head_dim, head_dim), jnp.float32),
    )
    incoming = entering_2((total_decay, total_state), "ctx", compose, identity)
    carried = incoming[1]
    block_id = 0
    entering = carried * (1.0 - resets[block_id])
    scaled_query = float_query[block_id] * jnp.exp(gate_sums[block_id])[..., None]
    outer_parts = [
        jnp.einsum("thd,hde->the", scaled_query, entering, precision=lax.Precision.HIGHEST)
    ]
    mixture = inner_part + jnp.stack(outer_parts)
    mean_square = jnp.mean(mixture * mixture, axis=-1, keepdims=True)
    rescaled_hidden = (
        mixture * lax.rsqrt(mean_square + 1e-06) * norm_gain.reshape(head_count, head_dim)
    )
    return rescaled_hidden.reshape(tok_rows, columns).astype(jnp.bfloat16)


def attend(my_queries, query_places, key_rows, value_rows, doc_ids, span_factor):
    all_rows, unit_heads, head_dim = key_rows.shape
    length = my_queries.shape[0]
    tile = min(512, length)
    span = tile * span_factor
    pad_key = jnp.concatenate(
        [
            jnp.zeros((WINDOW, unit_heads, head_dim), jnp.bfloat16),
            key_rows,
            jnp.zeros((span, unit_heads, head_dim), jnp.bfloat16),
        ]
    )
    pad_value = jnp.concatenate(
        [
            jnp.zeros((WINDOW, unit_heads, head_dim), jnp.bfloat16),
            value_rows,
            jnp.zeros((span, unit_heads, head_dim), jnp.bfloat16),
        ]
    )
    pad_docs = jnp.concatenate(
        [jnp.full((WINDOW,), -1, dtype=jnp.int32), doc_ids, jnp.full((span,), -1, dtype=jnp.int32)]
    )

    def one_tile(tile_index):
        tile_rows = lax.dynamic_slice_in_dim(my_queries, tile_index * tile, tile, 0)
        query_pos = lax.dynamic_slice_in_dim(query_places, tile_index * tile, tile, 0)
        first_pos = query_pos[0]
        key_block = lax.dynamic_slice_in_dim(pad_key, first_pos, WINDOW + span, 0)
        value_block = lax.dynamic_slice_in_dim(pad_value, first_pos, WINDOW + span, 0)
        key_docs = lax.dynamic_slice_in_dim(pad_docs, first_pos, WINDOW + span, 0)
        asker_documents = jnp.take(doc_ids, query_pos)
        key_pos = first_pos - WINDOW + jnp.arange(WINDOW + span, dtype=jnp.int32)
        allowed = (
            (key_pos[None, :] <= query_pos[:, None])
            & (key_pos[None, :] > query_pos[:, None] - WINDOW)
            & (key_docs[None, :] == asker_documents[:, None])
        )
        scores = jnp.einsum(
            "qhd,khd->hqk", tile_rows, key_block, preferred_element_type=jnp.float32
        ) * head_dim ** (-0.5)
        scores = jnp.where(allowed[None], scores, -1e30)
        row_peak = jnp.max(scores, axis=-1, keepdims=True)
        exponent = jnp.exp(scores - row_peak)
        weights = (exponent / jnp.sum(exponent, axis=-1, keepdims=True)).astype(jnp.bfloat16)
        return jnp.einsum(
            "hqk,khd->qhd", weights, value_block, preferred_element_type=jnp.float32
        ).astype(jnp.bfloat16)

    tiles_out = lax.map(one_tile, jnp.arange(length // tile, dtype=jnp.int32))
    return tiles_out.reshape(length, unit_heads, head_dim)


def body(gla_query, gla_key, gla_value, log_gates, norm_gain, attn_query, attn_key, doc_blocks):
    tok_rows, columns = attn_query.shape
    head_count = log_gates.shape[1]
    head_dim = columns // head_count
    devices = lax.axis_size("ctx")
    copies = max(1, devices // head_count)
    per_unit = max(1, head_count // devices)

    def to_heads(rows_in):
        spread_rows = rows_in.reshape(tok_rows, head_count, 1, head_dim)
        spread_rows = jnp.broadcast_to(spread_rows, (tok_rows, head_count, copies, head_dim))
        return spread_rows.reshape(tok_rows, devices, per_unit * head_dim)

    sent_query = to_heads(attn_query)
    gla_mixed = gla_layer(gla_query, gla_key, gla_value, log_gates, norm_gain, doc_blocks)
    moved_query, moved_key, moved_value = (
        lax.all_to_all(sent_query, "ctx", split_axis=1, concat_axis=0, tiled=True),
        lax.all_to_all(to_heads(attn_key), "ctx", split_axis=1, concat_axis=0, tiled=True),
        lax.all_to_all(to_heads(gla_mixed), "ctx", split_axis=1, concat_axis=0, tiled=True),
    )
    all_rows = devices * tok_rows
    doc_ends = jnp.cumsum(doc_blocks) * BLOCK
    positions = jnp.arange(all_rows, dtype=jnp.int32)
    doc_ids = jnp.sum((positions[:, None] >= doc_ends[None, :]).astype(jnp.int32), axis=1)
    local_replica = lax.axis_index("ctx") % copies
    part_count = 1
    my_part = 0
    length = all_rows // part_count
    first_row = my_part * length
    query_places = first_row + jnp.arange(length, dtype=jnp.int32)
    result = attend(moved_query, query_places, moved_key, moved_value, doc_ids, 1)
    result = jnp.where(local_replica == 0, result, jnp.zeros_like(result))
    outgoing = result.reshape(devices, tok_rows, 1, per_unit * head_dim)
    returned = lax.all_to_all(outgoing, "ctx", split_axis=0, concat_axis=2, tiled=True)
    returned = returned.reshape(tok_rows, head_count, copies, head_dim)
    attended = jnp.sum(returned.astype(jnp.float32), axis=2).astype(jnp.bfloat16)
    return (gla_mixed, attended.reshape(tok_rows, columns))


def solution(mesh):
    placed = (
        P(("grp", "ctx"), None),
        P(("grp", "ctx"), None),
        P(("grp", "ctx"), None),
        P(("grp", "ctx"), None),
        P(),
        P(("grp", "ctx"), None),
        P(("grp", "ctx"), None),
        P("grp"),
    )
    return jax.shard_map(
        body,
        mesh=mesh,
        in_specs=placed,
        out_specs=(P(("grp", "ctx"), None), P(("grp", "ctx"), None)),
        check_vma=False,
    )
```

profile of v0, /device:TPU:16, one launch (start us, length us, event | category | flops | bytes accessed | tf_op | source)
XLA Modules:
  0.0 1049.0 jit_solution(11235659924660422938)
XLA Ops:
  18.8 11.6 %all-to-all-start.2 = ((bf16[128,64,128]{2,0,1:T(8,128)(2,1)}), bf16[128,64,128]{2,0,1:T(8,128)(2,1)}, u32[]{:S(2)}, u32[]{:S(2)}) async-start(bf16[128,64,128]{2,0,1:T(8,128)(2,1)} %bitcast.155), calls=%async_computation.2 | async-start | bytes 4194304 | tf_op jit(solution)/shard_map/all_to_all | solution.py:157
  30.4 191.2 %all-gather = f32[64,1,32]{2,1,0:T(1,128)S(1)} all-gather(f32[1,1,32]{2,1,0:T(1,128)S(1)} %get-tuple-element.275), channel_id=2, replica_groups=mesh['grp'=2,'ctx'=64] {'ctx'}, dimensions={0}, use_global_device_ids=true | all-gather | bytes 8320 | tf_op jit(solution)/shard_map/all_gather | solution.py:12
  222.1 4.0 fusion.19
  226.1 325.2 %all-gather.4.cloned.1.call-done = f32[2048,128,128]{2,1,0:T(8,128)} async-done(((f32[32,128,128]{2,1,0:T(8,128)}), f32[2048,128,128]{2,1,0:T(8,128)}) %all-gather.4.cloned.1.call-update) | async-done | bytes 134217744 | tf_op jit(solution)/shard_map/all_gather | solution.py:12
  551.6 64.6 %while.27 = (s32[]{:T(128)}, f32[32,128,128]{2,1,0:T(8,128)S(1)}, s32[]{:T(128)}, f32[64,32]{1,0:T(8,128)S(1)}, f32[64,32,128,128]{3,2,1,0:T(8,128)}) while((s32[]{:T(128)}, f32[32,128,128]{2,1,0:T(8,128)S(1)}, s32[]{:T(128)}, f32[64,32]{1,0:T(8,128)S(1)}, f32[64,32,128,128]{3,2,1,0:T(8,128)}) %tuple.86), condition=%wide.region_4.5_spmd.clone, body=%wide.region_3.4_spmd.sunk.clone | while | flops 1048581 | bytes 6291951 | solution.py:20
  616.2 5.8 multiply_reduce_fusion
  626.7 70.3 %all-to-all-start = ((bf16[128,64,128]{2,0,1:T(8,128)(2,1)}), bf16[128,64,128]{2,0,1:T(8,128)(2,1)S(1)}, u32[]{:S(2)}, u32[]{:S(2)}) async-start(bf16[128,64,128]{2,0,1:T(8,128)(2,1)} %bitcast.156), calls=%async_computation | async-start | bytes 4194304 | tf_op jit(solution)/shard_map/all_to_all | solution.py:158
  699.7 25.1 %all-to-all-done = bf16[128,64,128]{2,0,1:T(8,128)(2,1)S(1)} async-done(((bf16[128,64,128]{2,0,1:T(8,128)(2,1)}), bf16[128,64,128]{2,0,1:T(8,128)(2,1)S(1)}, u32[]{:S(2)}, u32[]{:S(2)}) %all-to-all-start) | async-done | bytes 2097184 | tf_op jit(solution)/shard_map/all_to_all | solution.py:158
  724.8 3.4 broadcast_in_dim.102
  728.2 8.2 all-to-all-start.1
  736.3 12.7 %maximum_maximum_fusion.1 = (bf16[10752,1,128]{2,0,1:T(8,128)(2,1)}, bf16[10752,1,128]{2,0,1:T(8,128)(2,1)}) fusion(bf16[8192,1,128]{2,0,1:T(8,128)(2,1)} %bitcast.39, bf16[10752]{0:T(1024)(128)(2,1)S(1)} %pad.8.clone, bf16[10752]{0:T(1024)(128)(2,1)S(1)} %pad.6.clone, bf16[8192,1,128]{2,0,1:T(8,128)(2,1)S(1)} %bitcast.154), kind=kLoop, calls=%fused_computation.25 | loop fusion | flops 13762560 | bytes 9742336 | tf_op jit(solution)/shard_map/concatenate | solution.py:93
  749.1 13.3 %all-to-all-done.1 = bf16[128,64,128]{2,0,1:T(8,128)(2,1)} async-done(((bf16[128,64,128]{2,0,1:T(8,128)(2,1)}), bf16[128,64,128]{2,0,1:T(8,128)(2,1)}, u32[]{:S(2)}, u32[]{:S(2)}) %all-to-all-start.1) | async-done | bytes 2097184 | tf_op jit(solution)/shard_map/all_to_all | solution.py:156
  762.4 238.5 %while.28 = (s32[]{:T(128)}, bf16[16,512,1,128]{3,1,0,2:T(8,128)(2,1)}, s32[16]{0:T(128)S(1)}, s32[8192]{0:T(1024)S(1)}, bf16[10752,1,128]{2,0,1:T(8,128)(2,1)},...) while((s32[]{:T(128)}, ...), condition=%wide.region_10.11_spmd.clone, body=%wide.region_7.10_spmd.sunk.clone | while | flops 688201728 | bytes 17922296 | solution.py:136
  766.2 3.1 gather_fusion
  781.1 3.1 gather_fusion
  796.0 3.1 gather_fusion
  810.9 3.1 gather_fusion
  825.8 3.1 gather_fusion
  840.7 3.1 gather_fusion
  855.6 3.1 gather_fusion
  870.5 3.1 gather_fusion
  885.4 3.1 gather_fusion
  900.4 3.1 gather_fusion
  915.3 3.1 gather_fusion
  930.2 3.1 gather_fusion
  945.1 3.1 gather_fusion
  960.0 3.1 gather_fusion
  974.9 3.1 gather_fusion
  989.8 3.1 gather_fusion
  1000.9 3.1 broadcast_select_fusion
  1004.0 8.4 all-to-all-start.3
  1016.1 21.9 %all-to-all-done.3 = bf16[64,128,1,128]{3,1,2,0:T(8,128)(2,1)} async-done(((bf16[64,128,1,128]{3,1,2,0:T(8,128)(2,1)}), bf16[64,128,1,128]{3,1,2,0:T(8,128)(2,1)}, u32[]{:S(2)}, u32[]{:S(2)}) %all-to-all-start.3) | async-done | bytes 2097184 | tf_op jit(solution)/shard_map/all_to_all | solution.py:173
  (323 shorter events, 225.7 us)
Async XLA Ops:
  7.2 214.5 %copy-start = (bf16[128,4096]{1,0:T(8,128)(2,1)S(1)}, bf16[128,4096]{1,0:T(8,128)(2,1)}, u32[]{:S(2)}) copy-start(bf16[128,4096]{1,0:T(8,128)(2,1)} %param.12) | copy-start | bytes 3145732
  7.2 5.7 copy-start.3
  7.2 544.1 %all-gather.4.cloned.1.call-start = ((), (), s32[]{:S(2)}) async-start(), calls=%async_computation.4 | async-start | bytes 136314880 | tf_op jit(solution)/shard_map/all_gather | solution.py:12
  18.8 606.0 %all-to-all-start.2 = ((bf16[128,64,128]{2,0,1:T(8,128)(2,1)}), bf16[128,64,128]{2,0,1:T(8,128)(2,1)}, u32[]{:S(2)}, u32[]{:S(2)}) async-start(bf16[128,64,128]{2,0,1:T(8,128)(2,1)} %bitcast.155), calls=%async_computation.2 | async-start | bytes 4194304 | tf_op jit(solution)/shard_map/all_to_all | solution.py:157
  616.2 7.2 copy-start.4
  622.1 1.4 copy-start.1
  626.7 98.1 %all-to-all-start = ((bf16[128,64,128]{2,0,1:T(8,128)(2,1)}), bf16[128,64,128]{2,0,1:T(8,128)(2,1)S(1)}, u32[]{:S(2)}, u32[]{:S(2)}) async-start(bf16[128,64,128]{2,0,1:T(8,128)(2,1)} %bitcast.156), calls=%async_computation | async-start | bytes 4194304 | tf_op jit(solution)/shard_map/all_to_all | solution.py:158
  728.2 34.2 %all-to-all-start.1 = ((bf16[128,64,128]{2,0,1:T(8,128)(2,1)}), bf16[128,64,128]{2,0,1:T(8,128)(2,1)}, u32[]{:S(2)}, u32[]{:S(2)}) async-start(bf16[128,64,128]{2,0,1:T(8,128)(2,1)} %bitcast.157), calls=%async_computation.1 | async-start | bytes 4194304 | tf_op jit(solution)/shard_map/all_to_all | solution.py:156
  1004.0 8.4 copy-start.2
  1004.0 34.0 %all-to-all-start.3 = ((bf16[64,128,1,128]{3,1,2,0:T(8,128)(2,1)}), bf16[64,128,1,128]{3,1,2,0:T(8,128)(2,1)}, u32[]{:S(2)}, u32[]{:S(2)}) async-start(bf16[64,128,1,128]{3,1,2,0:T(8,128)(2,1)} %bitcast.158), calls=%async_computation.3 | async-start | bytes 4194304 | tf_op jit(solution)/shard_map/all_to_all | solution.py:173
Sparse Core Ops, SparseCore 0:
  15.6 535.6 all-gather.3
where the time goes:
time: 1060 us; the launch traced here: 1050 us
  waiting for transfers between devices  385 us (36%)
  blocking collectives  191 us (18%)
  local copies, waits for them, and re-layouts  102 us (10%)
  matrix products  102 us (10%)
  other arithmetic  101 us (10%)
  starting transfers between devices  98.4 us (9%)
  loops' own time  54 us (5%)
  between operations  14.9 us (1%)
    all_gather x1, waiting for transfers between devices, entering_2(): gathered = jax.tree.map(lambda a: lax.all_gather(a, axis), part)  325 us
    all_gather x1, blocking collectives, entering_2(): gathered = jax.tree.map(lambda a: lax.all_gather(a, axis), part)  191 us
    all_to_all x1, starting transfers between devices, body(): lax.all_to_all(to_heads(gla_mixed), 'ctx', split_axis=1, concat_axis=0, t...  70.3 us
    add x32, other arithmetic, compose(): later[0][:, None, None] * earlier[1] + later[1]  63.2 us
    another operation x1, loops' own time, attend(): tiles_out = lax.map(one_tile, jnp.arange(length // tile, dtype=jnp.int32))  52.9 us
    gather x16, local copies, waits for them, and re-layouts, one_tile(): asker_documents = jnp.take(doc_ids, query_pos)  50.3 us
    dot_general x16, matrix products, one_tile(): jnp.einsum('qhd,khd->hqk', tile_rows, key_block, preferred_element_type=j...  49.7 us
    dot_general x16, matrix products, one_tile(): jnp.einsum('hqk,khd->qhd', weights, value_block, preferred_element_type=j...  38.9 us
  transfers between devices with their start and end apart: 5, of which 4 were waited for; matrix products, arithmetic and copies ran while one was open for 9% of the time, Pallas kernels for 0%

commit v1 on v0

v1 whole, which is shorter than its diff:
```python
import functools
import math

import jax
import jax.numpy as jnp
from jax import lax
from jax.experimental import pallas as pl
from jax.experimental.pallas import tpu as pltpu
from jax.sharding import PartitionSpec as P

BLOCK = 128
DIM = 128
LOW = -1e30
HIGH = 1e30
SCALE = DIM ** (-0.5)
TO_EXP2 = SCALE / math.log(2.0)
MESH = pl.DeviceIdType.MESH
NT = (((1,), (1,)), ((), ()))
ROWS = DIM + 16


def columns_of(head):
    return pl.ds(pl.multiple_of(head * DIM, DIM), DIM)


def kernel(
    n,
    docs,
    gain,
    gates,
    gla_query,
    gla_key,
    gla_value,
    attn_query,
    attn_key,
    mixed,
    attended,
    gate_out,
    gate_in,
    key_in,
    value_in,
    query_in,
    attn_key_in,
    attn_query_in,
    states,
    decays,
    carry_out,
    carry_in,
    value_t,
    mixed_out,
    attended_out,
    score_t,
    send,
    recv,
    local,
):
    nb = n // 2
    halo = nb // 2
    place = lax.axis_index("ctx")
    half = lax.div(place, nb)
    rank = lax.rem(place, nb)
    base = half * nb
    turn = half * halo
    head = lax.rem(rank + turn, nb)
    partner = (1 - half) * nb + lax.rem(rank + halo, nb)

    lanes = lax.broadcasted_iota(jnp.int32, (BLOCK, BLOCK), 1)
    subs = lax.broadcasted_iota(jnp.int32, (BLOCK, BLOCK), 0)
    wide = jnp.concatenate(
        [gates[...], jnp.zeros((BLOCK, BLOCK - nb), jnp.float32)], axis=1
    )
    upto = jnp.where(subs <= lanes, 1.0, 0.0)
    sums = jnp.dot(
        wide.T, upto, precision=lax.Precision.HIGHEST, preferred_element_type=jnp.float32
    )
    for h in range(nb):
        gate_out[h] = jnp.broadcast_to(sums[h : h + 1], (8, BLOCK))

    barrier = pltpu.get_barrier_semaphore()

    def greet(i, _):
        pl.semaphore_signal(
            barrier, inc=1, device_id={"ctx": lax.rem(place + i, n)}, device_id_type=MESH
        )
        return 0

    lax.fori_loop(1, n, greet, 0)
    pl.semaphore_wait(barrier, n - 1)

    def push(src, dst, which, device):
        pltpu.make_async_remote_copy(
            src_ref=src,
            dst_ref=dst,
            send_sem=send.at[which],
            recv_sem=recv.at[which],
            device_id={"ctx": device},
            device_id_type=MESH,
        ).start()

    def spread(pick, dst, which):
        def one(i, _):
            push(
                pick(lax.rem(head + i, nb)), dst, which, base + lax.rem(rank + i, nb)
            )
            return 0

        lax.fori_loop(1, nb, one, 0)
        pltpu.make_async_copy(pick(head), dst, local.at[which]).start()

    def settle(ref, sem):
        pltpu.make_async_copy(ref, ref, sem).wait()

    def arrive(ref, one, which):
        settle(ref, recv.at[which])
        settle(one, local.at[which])

    def by_columns(src):
        return lambda h: src.at[:, columns_of(h)]

    spread(lambda h: gate_out.at[h], gate_in.at[rank], 0)
    spread(by_columns(gla_key), key_in.at[rank], 1)
    spread(by_columns(gla_value), value_in.at[rank], 2)
    spread(by_columns(gla_query), query_in.at[rank], 3)
    spread(by_columns(attn_key), attn_key_in.at[halo + rank], 4)
    gives_halo = jnp.logical_and(half == 0, rank >= halo)

    @pl.when(gives_halo)
    def _():
        def one(i, _):
            h = lax.rem(head + i, nb)
            push(
                attn_key.at[:, columns_of(h)],
                attn_key_in.at[rank - halo],
                5,
                nb + lax.rem(h + halo, nb),
            )
            return 0

        lax.fori_loop(0, nb, one, 0)

    spread(by_columns(attn_query), attn_query_in.at[rank], 6)

    value_t[:, DIM:, :] = jnp.ones((value_t.shape[0], ROWS - DIM, 2 * BLOCK), jnp.bfloat16)
    carry_zero = jnp.zeros((DIM, DIM), jnp.float32)

    @pl.when(half == 0)
    def _():
        attn_key_in[0:halo] = jnp.zeros((halo, BLOCK, DIM), jnp.bfloat16)
        value_t[0 : halo // 2, 0:DIM, :] = jnp.zeros(
            (halo // 2, DIM, 2 * BLOCK), jnp.bfloat16
        )
        carry_in[...] = carry_zero

    def doc_start(block):
        start = jnp.int32(0)
        best = jnp.int32(0)
        for d in range(docs.shape[0]):
            best = jnp.where(start <= block, start, best)
            start = start + docs[d]
        return best

    arrive(gate_in.at[0 : nb - 1], gate_in.at[0], 0)
    arrive(key_in.at[0 : nb - 1], key_in.at[0], 1)
    arrive(value_in.at[0 : nb - 1], value_in.at[0], 2)

    def gather_states(i, carried):
        state, decay = carried
        for u in range(2):
            b = 2 * i + u
            keep = jnp.where(doc_start(base + b) == base + b, 0.0, 1.0)
            row = gate_in[b][0:1]
            last = row[:, BLOCK - 1 : BLOCK]
            tails = jnp.exp(last - row)
            fade = jnp.exp(last)
            state = state * keep
            decay = decay * keep
            states[b] = state
            decays[b] = decay
            key_t = (key_in[b].astype(jnp.float32).T * tails).astype(jnp.bfloat16)
            state = state * fade + jnp.dot(
                key_t, value_in[b], preferred_element_type=jnp.float32
            )
            decay = decay * fade
        return state, decay

    state, _ = lax.fori_loop(
        0, nb // 2, gather_states, (carry_zero, jnp.ones((8, DIM), jnp.float32))
    )
    carry_out[...] = state

    @pl.when(half == 0)
    def _():
        push(carry_out, carry_in, 7, partner)

    arrive(query_in.at[0 : nb - 1], query_in.at[0], 3)

    @pl.when(half == 1)
    def _():
        settle(carry_in, recv.at[7])

    my_gain = gain[pl.ds(head, 1), :]
    causal = subs >= lanes

    def give_back(src, dst, which, block):
        @pl.when(block != rank)
        def _():
            push(src, dst, which, base + block)

        @pl.when(block == rank)
        def _():
            pltpu.make_async_copy(src, dst, local.at[which]).start()

    def mix(i, _):
        for u in range(2):
            b = 2 * i + u
            query = query_in[b]
            value = value_in[b]
            across = jnp.broadcast_to(gate_in[b][0:1], (BLOCK, BLOCK))
            down = across.T
            weight = jnp.where(
                causal, jnp.exp(jnp.where(causal, down - across, 0.0)), 0.0
            )
            scores = lax.dot_general(
                query, key_in[b], NT, preferred_element_type=jnp.float32
            )
            inner = jnp.dot(
                (scores * (weight * SCALE)).astype(jnp.bfloat16),
                value,
                preferred_element_type=jnp.float32,
            )
            entering = states[b] + decays[b][0:1] * carry_in[...]
            outer = jnp.dot(
                query, entering.astype(jnp.bfloat16), preferred_element_type=jnp.float32
            )
            total = inner + (jnp.exp(down) * SCALE) * outer
            square = jnp.mean(total * total, axis=-1, keepdims=True)
            result = total * lax.rsqrt(square + 1e-06) * my_gain
            mixed_out[b] = result.astype(jnp.bfloat16)
            value_t[halo // 2 + i, 0:DIM, u * BLOCK : (u + 1) * BLOCK] = result.T.astype(
                jnp.bfloat16
            )
            give_back(mixed_out.at[b], mixed.at[:, columns_of(head)], 8, b)

        @pl.when(jnp.logical_and(half == 0, i >= halo // 2))
        def _():
            push(
                value_t.at[halo // 2 + i, 0:DIM, :],
                value_t.at[i - halo // 2, 0:DIM, :],
                9,
                partner,
            )

        return 0

    lax.fori_loop(0, nb // 2, mix, 0)

    arrive(attn_key_in.at[halo : halo + nb - 1], attn_key_in.at[halo], 4)
    arrive(attn_query_in.at[0 : nb - 1], attn_query_in.at[0], 6)

    @pl.when(half == 1)
    def _():
        settle(attn_key_in.at[0:halo], recv.at[5])
        settle(value_t.at[0 : halo // 2, 0:DIM, :], recv.at[9])

    tile = 2 * BLOCK
    steps = halo // 2 + 1
    tile_lanes = lax.broadcasted_iota(jnp.int32, (tile, tile), 1)
    tile_subs = lax.broadcasted_iota(jnp.int32, (tile, tile), 0)
    first_lanes = lax.broadcasted_iota(jnp.int32, (8, tile), 1) < BLOCK

    def attend(i, _):
        query = attn_query_in[pl.ds(2 * i, 2)].reshape(tile, DIM)
        first = base + 2 * i
        start = jnp.where(first_lanes, doc_start(first), doc_start(first + 1))
        peak = jnp.full((8, tile), LOW, jnp.float32)
        for j in range(steps):
            keys = attn_key_in[pl.ds(2 * (i + j), 2)].reshape(tile, DIM)
            scores = lax.dot_general(keys, query, NT, preferred_element_type=jnp.float32)
            if j == 0:
                scores = jnp.where(tile_subs > tile_lanes, scores, LOW)
            if j == steps - 1:
                scores = jnp.where(tile_subs <= tile_lanes, scores, LOW)
            score_t[j] = scores
            for u in range(2):
                block = first - halo + 2 * j + u
                top = jnp.max(
                    scores[u * BLOCK : (u + 1) * BLOCK].reshape(BLOCK // 8, 8, tile), axis=0
                )
                peak = jnp.maximum(peak, jnp.where(start <= block, top, LOW))
        peak = jnp.max(peak, axis=0, keepdims=True)
        total = jnp.zeros((ROWS, tile), jnp.float32)
        for j in range(steps):
            parts = []
            for u in range(2):
                block = first - halo + 2 * j + u
                level = jnp.where(start[0:1] <= block, peak, HIGH)
                part = score_t[j, u * BLOCK : (u + 1) * BLOCK, :]
                parts.append(jnp.exp2((part - level) * TO_EXP2).astype(jnp.bfloat16))
            total = total + jnp.dot(
                value_t[i + j],
                jnp.concatenate(parts, axis=0),
                preferred_element_type=jnp.float32,
            )
        result = (total[0:DIM] / total[DIM : DIM + 1]).T.astype(jnp.bfloat16)
        for u in range(2):
            b = 2 * i + u
            attended_out[b] = result[u * BLOCK : (u + 1) * BLOCK]
            give_back(attended_out.at[b], attended.at[:, columns_of(head)], 10, b)
        return 0

    lax.fori_loop(0, nb // 2, attend, 0)

    most = columns_of(0)
    most = pl.ds(0, (nb - 1) * DIM)
    for which, out in ((8, mixed), (10, attended)):
        settle(out.at[:, most], recv.at[which])
        settle(out.at[:, columns_of(0)], local.at[which])
    settle(gate_out.at[0 : nb - 1], send.at[0])
    for which in (1, 2, 3, 4, 6, 8, 10):
        settle(key_in.at[0 : nb - 1], send.at[which])

    @pl.when(gives_halo)
    def _():
        settle(key_in.at[0:nb], send.at[5])

    @pl.when(half == 0)
    def _():
        settle(carry_out, send.at[7])
        settle(value_t.at[0 : halo // 2, 0:DIM, :], send.at[9])


def body(gla_query, gla_key, gla_value, log_gates, norm_gain, attn_query, attn_key, doc_blocks):
    n = lax.axis_size("ctx")
    nb = n // 2
    halo = nb // 2
    rows, columns = gla_query.shape
    out = jax.ShapeDtypeStruct((rows, columns), jnp.bfloat16)
    anywhere = pl.BlockSpec(memory_space=pl.ANY)
    vmem = pl.BlockSpec(memory_space=pltpu.VMEM)
    f32, bf16 = jnp.float32, jnp.bfloat16
    return pl.pallas_call(
        functools.partial(kernel, n),
        out_shape=(out, out),
        in_specs=[pl.BlockSpec(memory_space=pltpu.SMEM), vmem, vmem] + [anywhere] * 5,
        out_specs=(anywhere, anywhere),
        scratch_shapes=[
            pltpu.VMEM((nb, 8, BLOCK), f32),
            pltpu.VMEM((nb, 8, BLOCK), f32),
            pltpu.VMEM((nb, BLOCK, DIM), bf16),
            pltpu.VMEM((nb, BLOCK, DIM), bf16),
            pltpu.VMEM((nb, BLOCK, DIM), bf16),
            pltpu.VMEM((halo + nb, BLOCK, DIM), bf16),
            pltpu.VMEM((nb, BLOCK, DIM), bf16),
            pltpu.VMEM((nb, DIM, DIM), f32),
            pltpu.VMEM((nb, 8, DIM), f32),
            pltpu.VMEM((DIM, DIM), f32),
            pltpu.VMEM((DIM, DIM), f32),
            pltpu.VMEM(((halo + nb) // 2, ROWS, 2 * BLOCK), bf16),
            pltpu.VMEM((nb, BLOCK, DIM), bf16),
            pltpu.VMEM((nb, BLOCK, DIM), bf16),
            pltpu.VMEM((halo // 2 + 1, 2 * BLOCK, 2 * BLOCK), f32),
            pltpu.SemaphoreType.DMA((11,)),
            pltpu.SemaphoreType.DMA((11,)),
            pltpu.SemaphoreType.DMA((11,)),
        ],
        compiler_params=pltpu.CompilerParams(
            collective_id=0, has_side_effects=True, vmem_limit_bytes=40 * 2**20
        ),
    )(
        doc_blocks,
        norm_gain.reshape(nb, DIM),
        log_gates,
        gla_query,
        gla_key,
        gla_value,
        attn_query,
        attn_key,
    )


def solution(mesh):
    placed = P(("grp", "ctx"), None)
    return jax.shard_map(
        body,
        mesh=mesh,
        in_specs=(placed, placed, placed, placed, P(), placed, placed, P("grp")),
        out_specs=(placed, placed),
        check_vma=False,
    )
```

time: 1060 us -> 131 us (0.12)
  the two profiles are of different devices: /device:TPU:16 before, /device:TPU:104 now
where the time goes in v1:
time: 131 us; the launch traced here: 130 us
  Pallas kernels  121 us (92%)
  local copies, waits for them, and re-layouts  8.89 us (7%)
    pallas_call x1, Pallas kernels, body(): pl.pallas_call(functools.partial(kernel, n), out_shape=(out, out), in_spe...  121 us
    unnamed x17, local copies, waits for them, and re-layouts  8.89 us

profile of v1, /device:TPU:104, one launch (start us, length us, event | category | flops | bytes accessed | tf_op | source)
XLA Modules:
  0.0 130.2 jit_solution(12341665999751431401)
XLA Ops:
  0.6 0.0 copy-start.5
  0.6 0.0 copy-start.6
  0.7 0.8 copy.10.gates
  1.5 0.0 copy-done.5
  1.5 0.0 copy-done.6
  1.5 0.0 copy-start
  1.5 1.2 copy-done
  2.7 0.0 copy-start.1
  2.7 1.2 copy-done.1
  3.9 0.0 copy-start.2
  4.0 1.2 copy-done.2
  5.2 0.0 copy-start.3
  5.2 1.2 copy-done.3
  6.4 0.0 copy-start.4
  6.4 1.2 copy-done.4
  7.6 120.6 %shard_map.95 = (bf16[128,4096]{1,0:T(8,128)(2,1)S(1)}, bf16[128,4096]{1,0:T(8,128)(2,1)S(1)}) custom-call(s32[8]{0:T(128)S(1)} %copy-done.6, f32[32,128]{1,0:T(8,128)S(1)} %bitcast.1, f32[128,32]{1,0:T(8,128)S(1)} %copy.10.gates, bf16[128,4096]{1,0:T(8,128)(2,1)S(1)} %copy-done, bf16[128,4096]{1,0:T(8,128)(2,1)S(1)} %copy-done.1, ...), custom_call_target="tpu_custom_call" | custom-call | tf_op jit(solution)/shard_map/pallas_call | solution.py:341
  128.3 1.0 copy.13
  129.2 1.0 copy.14
Async XLA Ops:
  0.6 0.8 copy-start.5
  0.6 0.8 copy-start.6
  1.5 1.2 copy-start
  2.7 1.2 copy-start.1
  3.9 1.2 copy-start.2
  5.2 1.2 copy-start.3
  6.4 1.2 copy-start.4

commit v2 on v1

v2 whole, which is shorter than its diff:
```python
import functools
import math

import jax
import jax.numpy as jnp
from jax import lax
from jax.experimental import pallas as pl
from jax.experimental.pallas import tpu as pltpu
from jax.sharding import PartitionSpec as P

BLOCK = 128
DIM = 128
LOW = -1e30
HIGH = 1e30
SCALE = DIM ** (-0.5)
TO_EXP2 = SCALE / math.log(2.0)
MESH = pl.DeviceIdType.MESH
NT = (((1,), (1,)), ((), ()))
ROWS = DIM + 16


def columns_of(head):
    return pl.ds(pl.multiple_of(head * DIM, DIM), DIM)


def kernel(
    n,
    docs,
    gain,
    gates,
    gla_query,
    gla_key,
    gla_value,
    attn_query,
    attn_key,
    mixed,
    attended,
    own_query,
    own_key,
    own_value,
    sums,
    fade_out,
    fade_in,
    state_out,
    state_in,
    entering_out,
    entering_in,
    inner,
    mixed_out,
    value_out,
    value_t,
    attn_key_in,
    attn_query_in,
    score_t,
    weights_t,
    attended_out,
    send,
    recv,
    local,
):
    nb = n // 2
    halo = nb // 2
    part = DIM // 2
    place = lax.axis_index("ctx")
    half = lax.div(place, nb)
    rank = lax.rem(place, nb)
    base = half * nb
    turn = half * halo
    head = lax.rem(rank + turn, nb)
    partner = (1 - half) * nb + lax.rem(rank + halo, nb)
    barrier = pltpu.get_barrier_semaphore()

    def greet(i, _):
        pl.semaphore_signal(
            barrier, inc=1, device_id={"ctx": lax.rem(place + i, n)}, device_id_type=MESH
        )
        return 0

    lax.fori_loop(1, n, greet, 0)

    def push(src, dst, which, device):
        pltpu.make_async_remote_copy(
            src_ref=src,
            dst_ref=dst,
            send_sem=send.at[which],
            recv_sem=recv.at[which],
            device_id={"ctx": device},
            device_id_type=MESH,
        ).start()

    def push_any(src, dst, which, device):
        @pl.when(device != place)
        def _():
            push(src, dst, which, device)

        @pl.when(device == place)
        def _():
            pltpu.make_async_copy(src, dst, local.at[which]).start()

    def settle(ref, sem):
        pltpu.make_async_copy(ref, ref, sem).wait()

    def arrive(ref, one, which):
        settle(ref, recv.at[which])
        settle(one, local.at[which])

    pltpu.make_async_copy(gla_key, own_key, local.at[9]).start()
    pltpu.make_async_copy(gla_value, own_value, local.at[10]).start()
    pltpu.make_async_copy(gla_query, own_query, local.at[11]).start()

    lanes = lax.broadcasted_iota(jnp.int32, (BLOCK, BLOCK), 1)
    subs = lax.broadcasted_iota(jnp.int32, (BLOCK, BLOCK), 0)
    upto = jnp.where(subs <= lanes, 1.0, 0.0)
    summed = jnp.dot(
        gates[...], upto, precision=lax.Precision.HIGHEST, preferred_element_type=jnp.float32
    )
    for h in range(nb):
        sums[h] = summed[h : h + 1]
        fade_out[h] = jnp.exp(jnp.broadcast_to(summed[h : h + 1, BLOCK - 1 :], (1, BLOCK)))
    value_t[:, DIM:, :] = jnp.ones((value_t.shape[0], ROWS - DIM, BLOCK), jnp.bfloat16)

    @pl.when(half == 0)
    def _():
        attn_key_in[0:halo] = jnp.zeros((halo, BLOCK, DIM), jnp.bfloat16)
        value_t[0:halo, 0:DIM, :] = jnp.zeros((halo, DIM, BLOCK), jnp.bfloat16)

    def doc_start(block):
        start = jnp.int32(0)
        best = jnp.int32(0)
        for d in range(docs.shape[0]):
            best = jnp.where(start <= block, start, best)
            start = start + docs[d]
        return best

    settle(own_key, local.at[9])
    settle(own_value, local.at[10])
    pl.semaphore_wait(barrier, n - 1)

    def gained(i, _):
        for u in range(2):
            h = lax.rem(rank + 2 * i + u, nb)
            row = sums[h]
            tails = jnp.exp(row[:, BLOCK - 1 :] - row)
            key_t = own_key[:, columns_of(h)].astype(jnp.float32).T * tails
            state = jnp.dot(
                key_t.astype(jnp.bfloat16),
                own_value[:, columns_of(h)],
                preferred_element_type=jnp.float32,
            )
            state_out[h] = state.astype(jnp.bfloat16)
            for w in range(2):
                owner = h + w * nb
                push_any(fade_out.at[h], fade_in.at[place], 0, owner)
                push_any(
                    state_out.at[h, w * part : (w + 1) * part], state_in.at[place], 1, owner
                )
        return 0

    lax.fori_loop(0, nb // 2, gained, 0)

    def spread(src, dst, which):
        def one(i, _):
            h = lax.rem(head + i, nb)
            push(src.at[:, columns_of(h)], dst, which, base + lax.rem(rank + i, nb))
            return 0

        lax.fori_loop(1, nb, one, 0)
        pltpu.make_async_copy(src.at[:, columns_of(head)], dst, local.at[which]).start()

    spread(attn_key, attn_key_in.at[halo + rank], 2)
    settle(own_query, local.at[11])
    causal = subs >= lanes

    def within(i, _):
        for u in range(2):
            h = 2 * i + u
            across = jnp.broadcast_to(sums[h], (BLOCK, BLOCK))
            down = across.T
            weight = jnp.where(
                causal, jnp.exp(jnp.where(causal, down - across, 0.0)), 0.0
            )
            scores = lax.dot_general(
                own_query[:, columns_of(h)],
                own_key[:, columns_of(h)],
                NT,
                preferred_element_type=jnp.float32,
            )
            inner[h] = jnp.dot(
                (scores * (weight * SCALE)).astype(jnp.bfloat16),
                own_value[:, columns_of(h)],
                preferred_element_type=jnp.float32,
            )
        return 0

    lax.fori_loop(0, nb // 2, within, 0)

    arrive(fade_in.at[0 : n - 1], fade_in.at[0], 0)
    arrive(state_in.at[0 : n - 1], state_in.at[0], 1)

    def scan(i, state):
        for u in range(2):
            b = 2 * i + u
            state = state * jnp.where(doc_start(b) == b, 0.0, 1.0)
            entering_out[b] = state.astype(jnp.bfloat16)
            state = state * fade_in[b] + state_in[b].astype(jnp.float32)
        return state

    lax.fori_loop(0, nb, scan, jnp.zeros((part, DIM), jnp.float32))

    mine = entering_in.at[2 * rank + half]

    def enter(i, _):
        device = lax.rem(place + i, n)
        push(entering_out.at[device], mine, 3, device)
        return 0

    lax.fori_loop(1, n, enter, 0)
    pltpu.make_async_copy(entering_out.at[place], mine, local.at[3]).start()

    spread(attn_query, attn_query_in.at[rank], 4)
    arrive(attn_key_in.at[halo : halo + nb - 1], attn_key_in.at[halo], 2)

    @pl.when(half == 0)
    def _():
        push(attn_key_in.at[nb : nb + halo], attn_key_in.at[0:halo], 5, partner)

    arrive(entering_in.at[0 : n - 1], entering_in.at[0], 3)

    def mix(i, _):
        for u in range(2):
            h = lax.rem(head + 2 * i + u, nb)
            down = jnp.broadcast_to(sums[h], (BLOCK, BLOCK)).T
            entering = entering_in[pl.ds(2 * h, 2)].reshape(DIM, DIM)
            outer = jnp.dot(
                own_query[:, columns_of(h)], entering, preferred_element_type=jnp.float32
            )
            total = inner[h] + (jnp.exp(down) * SCALE) * outer
            square = jnp.mean(total * total, axis=-1, keepdims=True)
            result = total * lax.rsqrt(square + 1e-06) * gain[pl.ds(h, 1), :]
            value_out[h] = result.T.astype(jnp.bfloat16)
            push_any(
                value_out.at[h],
                value_t.at[halo + rank, 0:DIM],
                6,
                base + lax.rem(h + turn, nb),
            )
            mixed_out[h] = result.astype(jnp.bfloat16)
            pltpu.make_async_copy(
                mixed_out.at[h], mixed.at[:, columns_of(h)], local.at[9]
            ).start()
        return 0

    lax.fori_loop(0, nb // 2, mix, 0)

    arrive(attn_query_in.at[0 : nb - 1], attn_query_in.at[0], 4)

    @pl.when(half == 1)
    def _():
        settle(attn_key_in.at[0:halo], recv.at[5])

    tile = 2 * BLOCK
    tiles = nb // 2
    steps = halo // 2 + 1
    tile_lanes = lax.broadcasted_iota(jnp.int32, (tile, tile), 1)
    tile_subs = lax.broadcasted_iota(jnp.int32, (tile, tile), 0)
    first_lanes = lax.broadcasted_iota(jnp.int32, (8, tile), 1) < BLOCK

    def weigh(i, _):
        query = attn_query_in[pl.ds(2 * i, 2)].reshape(tile, DIM)
        first = base + 2 * i
        start = jnp.where(first_lanes, doc_start(first), doc_start(first + 1))
        peak = jnp.full((8, tile), LOW, jnp.float32)
        for j in range(steps):
            keys = attn_key_in[pl.ds(2 * (i + j), 2)].reshape(tile, DIM)
            scores = lax.dot_general(keys, query, NT, preferred_element_type=jnp.float32)
            if j == 0:
                scores = jnp.where(tile_subs > tile_lanes, scores, LOW)
            if j == steps - 1:
                scores = jnp.where(tile_subs <= tile_lanes, scores, LOW)
            score_t[j] = scores
            for u in range(2):
                block = first - halo + 2 * j + u
                top = jnp.max(
                    scores[u * BLOCK : (u + 1) * BLOCK].reshape(BLOCK // 8, 8, tile), axis=0
                )
                peak = jnp.maximum(peak, jnp.where(start <= block, top, LOW))
        peak = jnp.max(peak, axis=0, keepdims=True)
        for j in range(steps):
            for u in range(2):
                block = first - halo + 2 * j + u
                level = jnp.where(start[0:1] <= block, peak, HIGH)
                span = slice(u * BLOCK, (u + 1) * BLOCK)
                weights_t[i, j, span, :] = jnp.exp2(
                    (score_t[j, span, :] - level) * TO_EXP2
                ).astype(jnp.bfloat16)
        return 0

    lax.fori_loop(0, tiles, weigh, 0)

    arrive(value_t.at[halo : halo + nb - 1, 0:DIM], value_t.at[halo, 0:DIM], 6)

    @pl.when(half == 0)
    def _():
        push(value_t.at[nb : nb + halo, 0:DIM], value_t.at[0:halo, 0:DIM], 7, partner)

    def attend(i, _):
        total = jnp.zeros((ROWS, tile), jnp.float32)
        for j in range(steps):
            at = 2 * (i + j)
            total = total + jnp.dot(
                jnp.concatenate([value_t[at], value_t[at + 1]], axis=1),
                weights_t[i, j],
                preferred_element_type=jnp.float32,
            )
        result = (total[0:DIM] / total[DIM : DIM + 1]).T.astype(jnp.bfloat16)
        for u in range(2):
            b = 2 * i + u
            attended_out[b] = result[u * BLOCK : (u + 1) * BLOCK]
            push_any(attended_out.at[b], attended.at[:, columns_of(head)], 8, base + b)
        return 0

    lax.fori_loop(tiles // 2, tiles, attend, 0)

    @pl.when(half == 1)
    def _():
        settle(value_t.at[0:halo, 0:DIM], recv.at[7])

    lax.fori_loop(0, tiles // 2, attend, 0)

    settle(mixed, local.at[9])
    arrive(attended.at[:, pl.ds(0, (nb - 1) * DIM)], attended.at[:, columns_of(0)], 8)
    settle(fade_in.at[0 : n - 1], send.at[0])
    settle(state_in.at[0 : n - 1], send.at[1])
    settle(entering_in.at[0 : n - 1], send.at[3])
    for which in (2, 4, 6, 8):
        settle(value_out.at[0 : nb - 1], send.at[which])

    @pl.when(half == 0)
    def _():
        settle(value_out.at[0:halo], send.at[5])
        settle(value_out.at[0:halo], send.at[7])


def body(gla_query, gla_key, gla_value, log_gates, norm_gain, attn_query, attn_key, doc_blocks):
    n = lax.axis_size("ctx")
    nb = n // 2
    halo = nb // 2
    rows, columns = gla_query.shape
    out = jax.ShapeDtypeStruct((rows, columns), jnp.bfloat16)
    anywhere = pl.BlockSpec(memory_space=pl.ANY)
    vmem = pl.BlockSpec(memory_space=pltpu.VMEM)
    f32, bf16 = jnp.float32, jnp.bfloat16
    square = (BLOCK, DIM)
    tile = 2 * BLOCK
    steps = halo // 2 + 1
    return pl.pallas_call(
        functools.partial(kernel, n),
        out_shape=(out, out),
        in_specs=[pl.BlockSpec(memory_space=pltpu.SMEM), vmem, vmem] + [anywhere] * 5,
        out_specs=(anywhere, anywhere),
        scratch_shapes=[
            pltpu.VMEM((rows, columns), bf16),
            pltpu.VMEM((rows, columns), bf16),
            pltpu.VMEM((rows, columns), bf16),
            pltpu.VMEM((nb, 1, BLOCK), f32),
            pltpu.VMEM((nb, 1, BLOCK), f32),
            pltpu.VMEM((n, 1, BLOCK), f32),
            pltpu.VMEM((nb, DIM, DIM), bf16),
            pltpu.VMEM((n, DIM // 2, DIM), bf16),
            pltpu.VMEM((n, DIM // 2, DIM), bf16),
            pltpu.VMEM((n, DIM // 2, DIM), bf16),
            pltpu.VMEM((nb, *square), f32),
            pltpu.VMEM((nb, *square), bf16),
            pltpu.VMEM((nb, *square), bf16),
            pltpu.VMEM((halo + nb, ROWS, BLOCK), bf16),
            pltpu.VMEM((halo + nb, *square), bf16),
            pltpu.VMEM((nb, *square), bf16),
            pltpu.VMEM((steps, tile, tile), f32),
            pltpu.VMEM((nb // 2, steps, tile, tile), bf16),
            pltpu.VMEM((nb, *square), bf16),
            pltpu.SemaphoreType.DMA((12,)),
            pltpu.SemaphoreType.DMA((12,)),
            pltpu.SemaphoreType.DMA((12,)),
        ],
        compiler_params=pltpu.CompilerParams(
            collective_id=0, has_side_effects=True, vmem_limit_bytes=60 * 2**20
        ),
    )(
        doc_blocks,
        norm_gain.reshape(nb, DIM),
        log_gates.T,
        gla_query,
        gla_key,
        gla_value,
        attn_query,
        attn_key,
    )


def solution(mesh):
    placed = P(("grp", "ctx"), None)
    return jax.shard_map(
        body,
        mesh=mesh,
        in_specs=(placed, placed, placed, placed, P(), placed, placed, P("grp")),
        out_specs=(placed, placed),
        check_vma=False,
    )
```

time: 131 us -> 106 us (0.81)
  the two profiles are of different devices: /device:TPU:104 before, /device:TPU:16 now
where the time goes in v2:
time: 106 us
  Pallas kernels  102 us (96%)
  local copies, waits for them, and re-layouts  3.35 us (3%)
    pallas_call x1, Pallas kernels, body(): pl.pallas_call(functools.partial(kernel, n), out_shape=(out, out), in_spe...  102 us
    unnamed x4, local copies, waits for them, and re-layouts  3.35 us

profile of v2, /device:TPU:16, one launch (start us, length us, event | category | flops | bytes accessed | tf_op | source)
XLA Modules:
  0.0 106.3 jit_solution(15195619795444804404)
XLA Ops:
  0.6 102.3 %shard_map.95 = (bf16[128,4096]{1,0:T(8,128)(2,1)}, bf16[128,4096]{1,0:T(8,128)(2,1)}) custom-call(s32[8]{0:T(128)} %docs.1, f32[32,128]{1,0:T(8,128)} %bitcast.2, f32[32,128]{1,0:T(8,128)} %bitcast.3, bf16[128,4096]{1,0:T(8,128)(2,1)} %gla_query.1, bf16[128,4096]{1,0:T(8,128)(2,1)} %gla_key.1, bf16[128,4096]{1,0:T(8,128)(2,1)} %gla_value.1, ...), custom_call_target="tpu_custom_call" | custom-call | tf_op jit(solution)/shard_map/pallas_call | solution.py:356
  102.9 0.0 copy-start
  103.0 2.4 %copy.12 = bf16[128,4096]{1,0:T(8,128)(2,1)} copy(bf16[128,4096]{1,0:T(8,128)(2,1)} %get-tuple-element.4) | data formatting | bytes 2097152
  105.3 0.0 copy-done
  105.3 1.0 copy.13
Async XLA Ops:
  102.9 2.4 %copy-start = (bf16[128,4096]{1,0:T(8,128)(2,1)S(1)}, bf16[128,4096]{1,0:T(8,128)(2,1)}, u32[]{:S(2)}) copy-start(bf16[128,4096]{1,0:T(8,128)(2,1)} %get-tuple-element.5) | copy-start | bytes 3145732

commit v3 on v2

--- a/solution.py
+++ b/solution.py
@@ -17,6 +17,8 @@
 MESH = pl.DeviceIdType.MESH
 NT = (((1,), (1,)), ((), ()))
 ROWS = DIM + 16
+STRIDE = 5
+EARLY = 8
 
 
 def columns_of(head):
@@ -38,6 +40,8 @@
     own_query,
     own_key,
     own_value,
+    own_value_t,
+    gain_t,
     sums,
     fade_out,
     fade_in,
@@ -57,6 +61,7 @@
     send,
     recv,
     local,
+    recv_value,
 ):
     nb = n // 2
     halo = nb // 2
@@ -108,6 +113,19 @@
     pltpu.make_async_copy(gla_value, own_value, local.at[10]).start()
     pltpu.make_async_copy(gla_query, own_query, local.at[11]).start()
 
+    pl.semaphore_wait(barrier, n - 1)
+
+    def spread(src, dst, which):
+        def one(i, _):
+            h = lax.rem(head + STRIDE * i, nb)
+            push(src.at[:, columns_of(h)], dst, which, base + lax.rem(rank + STRIDE * i, nb))
+            return 0
+
+        lax.fori_loop(1, nb, one, 0)
+        pltpu.make_async_copy(src.at[:, columns_of(head)], dst, local.at[which]).start()
+
+    spread(attn_key, attn_key_in.at[halo + rank], 2)
+
     lanes = lax.broadcasted_iota(jnp.int32, (BLOCK, BLOCK), 1)
     subs = lax.broadcasted_iota(jnp.int32, (BLOCK, BLOCK), 0)
     upto = jnp.where(subs <= lanes, 1.0, 0.0)
@@ -134,17 +152,17 @@
 
     settle(own_key, local.at[9])
     settle(own_value, local.at[10])
-    pl.semaphore_wait(barrier, n - 1)
 
     def gained(i, _):
         for u in range(2):
-            h = lax.rem(rank + 2 * i + u, nb)
+            h = lax.rem(rank + STRIDE * (2 * i + u), nb)
             row = sums[h]
             tails = jnp.exp(row[:, BLOCK - 1 :] - row)
-            key_t = own_key[:, columns_of(h)].astype(jnp.float32).T * tails
+            turned = own_value[:, columns_of(h)].astype(jnp.float32).T
+            own_value_t[h] = turned.astype(jnp.bfloat16)
             state = jnp.dot(
-                key_t.astype(jnp.bfloat16),
-                own_value[:, columns_of(h)],
+                (turned * tails).astype(jnp.bfloat16),
+                own_key[:, columns_of(h)],
                 preferred_element_type=jnp.float32,
             )
             state_out[h] = state.astype(jnp.bfloat16)
@@ -158,16 +176,7 @@
 
     lax.fori_loop(0, nb // 2, gained, 0)
 
-    def spread(src, dst, which):
-        def one(i, _):
-            h = lax.rem(head + i, nb)
-            push(src.at[:, columns_of(h)], dst, which, base + lax.rem(rank + i, nb))
-            return 0
-
-        lax.fori_loop(1, nb, one, 0)
-        pltpu.make_async_copy(src.at[:, columns_of(head)], dst, local.at[which]).start()
-
-    spread(attn_key, attn_key_in.at[halo + rank], 2)
+    spread(attn_query, attn_query_in.at[rank], 4)
     settle(own_query, local.at[11])
     causal = subs >= lanes
 
@@ -185,14 +194,22 @@
                 NT,
                 preferred_element_type=jnp.float32,
             )
-            inner[h] = jnp.dot(
+            inner[h] = lax.dot_general(
+                own_value_t[h],
                 (scores * (weight * SCALE)).astype(jnp.bfloat16),
-                own_value[:, columns_of(h)],
+                NT,
                 preferred_element_type=jnp.float32,
             )
+            gain_t[h] = jnp.broadcast_to(gain[pl.ds(h, 1), :], (BLOCK, DIM)).T
         return 0
 
     lax.fori_loop(0, nb // 2, within, 0)
+    arrive(attn_key_in.at[halo : halo + nb - 1], attn_key_in.at[halo], 2)
+
+    @pl.when(half == 0)
+    def _():
+        push(attn_key_in.at[nb : nb + halo], attn_key_in.at[0:halo], 5, partner)
+
 
     arrive(fade_in.at[0 : n - 1], fade_in.at[0], 0)
     arrive(state_in.at[0 : n - 1], state_in.at[0], 1)
@@ -210,53 +227,14 @@
     mine = entering_in.at[2 * rank + half]
 
     def enter(i, _):
-        device = lax.rem(place + i, n)
+        device = lax.rem(place + STRIDE * i, n)
         push(entering_out.at[device], mine, 3, device)
         return 0
 
     lax.fori_loop(1, n, enter, 0)
     pltpu.make_async_copy(entering_out.at[place], mine, local.at[3]).start()
 
-    spread(attn_query, attn_query_in.at[rank], 4)
-    arrive(attn_key_in.at[halo : halo + nb - 1], attn_key_in.at[halo], 2)
-
-    @pl.when(half == 0)
-    def _():
-        push(attn_key_in.at[nb : nb + halo], attn_key_in.at[0:halo], 5, partner)
-
-    arrive(entering_in.at[0 : n - 1], entering_in.at[0], 3)
-
-    def mix(i, _):
-        for u in range(2):
-            h = lax.rem(head + 2 * i + u, nb)
-            down = jnp.broadcast_to(sums[h], (BLOCK, BLOCK)).T
-            entering = entering_in[pl.ds(2 * h, 2)].reshape(DIM, DIM)
-            outer = jnp.dot(
-                own_query[:, columns_of(h)], entering, preferred_element_type=jnp.float32
-            )
-            total = inner[h] + (jnp.exp(down) * SCALE) * outer
-            square = jnp.mean(total * total, axis=-1, keepdims=True)
-            result = total * lax.rsqrt(square + 1e-06) * gain[pl.ds(h, 1), :]
-            value_out[h] = result.T.astype(jnp.bfloat16)
-            push_any(
-                value_out.at[h],
-                value_t.at[halo + rank, 0:DIM],
-                6,
-                base + lax.rem(h + turn, nb),
-            )
-            mixed_out[h] = result.astype(jnp.bfloat16)
-            pltpu.make_async_copy(
-                mixed_out.at[h], mixed.at[:, columns_of(h)], local.at[9]
-            ).start()
-        return 0
-
-    lax.fori_loop(0, nb // 2, mix, 0)
-
     arrive(attn_query_in.at[0 : nb - 1], attn_query_in.at[0], 4)
-
-    @pl.when(half == 1)
-    def _():
-        settle(attn_key_in.at[0:halo], recv.at[5])
 
     tile = 2 * BLOCK
     tiles = nb // 2
@@ -265,7 +243,8 @@
     tile_subs = lax.broadcasted_iota(jnp.int32, (tile, tile), 0)
     first_lanes = lax.broadcasted_iota(jnp.int32, (8, tile), 1) < BLOCK
 
-    def weigh(i, _):
+    def weigh(k, _):
+        i = lax.rem(k + tiles // 2, tiles)
         query = attn_query_in[pl.ds(2 * i, 2)].reshape(tile, DIM)
         first = base + 2 * i
         start = jnp.where(first_lanes, doc_start(first), doc_start(first + 1))
@@ -295,15 +274,91 @@
                 ).astype(jnp.bfloat16)
         return 0
 
-    lax.fori_loop(0, tiles, weigh, 0)
-
-    arrive(value_t.at[halo : halo + nb - 1, 0:DIM], value_t.at[halo, 0:DIM], 6)
-
-    @pl.when(half == 0)
+    lax.fori_loop(0, EARLY, weigh, 0)
+    arrive(entering_in.at[0 : n - 1], entering_in.at[0], 3)
+
+    def mix(i, _):
+        for u in range(2):
+            h = lax.rem(head + STRIDE * (2 * i + u), nb)
+            entering = entering_in[pl.ds(2 * h, 2)].reshape(DIM, DIM)
+            outer = lax.dot_general(
+                entering,
+                own_query[:, columns_of(h)],
+                NT,
+                preferred_element_type=jnp.float32,
+            )
+            total = inner[h] + (jnp.exp(sums[h]) * SCALE) * outer
+            square = jnp.mean(total * total, axis=0, keepdims=True)
+            value_out[h] = (total * lax.rsqrt(square + 1e-06) * gain_t[h]).astype(
+                jnp.bfloat16
+            )
+            device = base + lax.rem(h + turn, nb)
+            block = value_t.at[halo + rank, 0:DIM]
+
+            @pl.when(device != place)
+            def _():
+                pltpu.make_async_remote_copy(
+                    src_ref=value_out.at[h],
+                    dst_ref=block,
+                    send_sem=send.at[6],
+                    recv_sem=recv_value.at[rank],
+                    device_id={"ctx": device},
+                    device_id_type=MESH,
+                ).start()
+
+            @pl.when(device == place)
+            def _():
+                pltpu.make_async_copy(value_out.at[h], block, local.at[6]).start()
+
+        return 0
+
+    lax.fori_loop(0, nb // 2, mix, 0)
+
+    @pl.when(half == 1)
     def _():
-        push(value_t.at[nb : nb + halo, 0:DIM], value_t.at[0:halo, 0:DIM], 7, partner)
-
-    def attend(i, _):
+        settle(attn_key_in.at[0:halo], recv.at[5])
+
+    late = tiles - EARLY
+    per_tile = nb // late
+
+    def take(i):
+        source = lax.rem(rank + nb - lax.rem(STRIDE * i, nb), nb)
+        block = value_t.at[halo + source, 0:DIM]
+
+        @pl.when(i == 0)
+        def _():
+            settle(block, local.at[6])
+
+        @pl.when(i > 0)
+        def _():
+            settle(block, recv_value.at[source])
+
+        @pl.when(jnp.logical_and(half == 0, source >= halo))
+        def _():
+            pltpu.make_async_remote_copy(
+                src_ref=block,
+                dst_ref=value_t.at[source - halo, 0:DIM],
+                send_sem=send.at[7],
+                recv_sem=recv.at[7],
+                device_id={"ctx": partner},
+                device_id_type=MESH,
+            ).start()
+
+    def weigh_and_take(k, _):
+        weigh(EARLY + k, 0)
+        for u in range(per_tile):
+            h = k * per_tile + u
+            mixed_out[h] = value_out[h].T
+            pltpu.make_async_copy(
+                mixed_out.at[h], mixed.at[:, columns_of(h)], local.at[9]
+            ).start()
+            take(h)
+        return 0
+
+    lax.fori_loop(0, late, weigh_and_take, 0)
+
+    def attend(k, _):
+        i = lax.div(k, tiles // 2) * (tiles // 2) + lax.rem(k + rank, tiles // 2)
         total = jnp.zeros((ROWS, tile), jnp.float32)
         for j in range(steps):
             at = 2 * (i + j)
@@ -356,12 +411,14 @@
     return pl.pallas_call(
         functools.partial(kernel, n),
         out_shape=(out, out),
-        in_specs=[pl.BlockSpec(memory_space=pltpu.SMEM), vmem, vmem] + [anywhere] * 5,
+        in_specs=[pl.BlockSpec(memory_space=pltpu.SMEM), vmem, vmem] + [pl.BlockSpec(memory_space=pltpu.HBM)] * 5,
         out_specs=(anywhere, anywhere),
         scratch_shapes=[
             pltpu.VMEM((rows, columns), bf16),
             pltpu.VMEM((rows, columns), bf16),
             pltpu.VMEM((rows, columns), bf16),
+            pltpu.VMEM((nb, *square), bf16),
+            pltpu.VMEM((nb, *square), f32),
             pltpu.VMEM((nb, 1, BLOCK), f32),
             pltpu.VMEM((nb, 1, BLOCK), f32),
             pltpu.VMEM((n, 1, BLOCK), f32),
@@ -381,9 +438,10 @@
             pltpu.SemaphoreType.DMA((12,)),
             pltpu.SemaphoreType.DMA((12,)),
             pltpu.SemaphoreType.DMA((12,)),
+            pltpu.SemaphoreType.DMA((nb,)),
         ],
         compiler_params=pltpu.CompilerParams(
-            collective_id=0, has_side_effects=True, vmem_limit_bytes=60 * 2**20
+            collective_id=0, has_side_effects=True, vmem_limit_bytes=50 * 2**20
         ),
     )(
         doc_blocks,

time: 106 us -> 101 us (0.953)
  Pallas kernels: 102 us -> 94.8 us
  local copies, waits for them, and re-layouts: 3.35 us -> 5.25 us
    pallas_call x1, Pallas kernels: 102 us -> 94.8 us  [body(): pl.pallas_call(functools.partial(kernel, n), out_shape=(out, out), in_spe...]
    unnamed x4 -> x10, local copies, waits for them, and re-layouts: 3.35 us -> 5.25 us
where the time goes in v3:
time: 101 us
  Pallas kernels  94.8 us (94%)
  local copies, waits for them, and re-layouts  5.25 us (5%)
    pallas_call x1, Pallas kernels, body(): pl.pallas_call(functools.partial(kernel, n), out_shape=(out, out), in_spe...  94.8 us
    unnamed x10, local copies, waits for them, and re-layouts  5.25 us

profile of v3, /device:TPU:16, one launch (start us, length us, event | category | flops | bytes accessed | tf_op | source)
XLA Modules:
  0.0 100.7 jit_solution(18438326709253664913)
XLA Ops:
  0.6 0.0 copy-start.3
  0.6 0.6 copy-done.3
  1.3 0.0 copy-start
  1.3 1.2 %copy-done = bf16[128,4096]{1,0:T(8,128)(2,1)S(1)} copy-done((bf16[128,4096]{1,0:T(8,128)(2,1)S(1)}, bf16[128,4096]{1,0:T(8,128)(2,1)}, u32[]{:S(2)}) %copy-start) | copy-done | bytes 1048600
  2.5 0.0 copy-start.1
  2.5 0.7 copy-done.1
  3.2 0.0 copy-start.2
  3.2 0.7 copy-done.2
  4.0 94.8 %shard_map.95 = (bf16[128,4096]{1,0:T(8,128)(2,1)S(1)}, bf16[128,4096]{1,0:T(8,128)(2,1)S(1)}) custom-call(s32[8]{0:T(128)S(1)} %copy-done.3, f32[32,128]{1,0:T(8,128)S(1)} %bitcast.2, f32[32,128]{1,0:T(8,128)S(1)} %bitcast.3, bf16[128,4096]{1,0:T(8,128)(2,1)S(1)} %copy-done, bf16[128,4096]{1,0:T(8,128)(2,1)} %gla_key.1, bf16[128,4096]{1,0:T(8,128)(2,1)} %gla_value.1, ...), custom_call_target="tpu_custom_call" | custom-call | tf_op jit(solution)/shard_map/pallas_call | solution.py:411
  98.7 1.0 copy.12
  99.7 1.0 copy.13
Async XLA Ops:
  0.6 0.7 copy-start.3
  1.3 1.2 %copy-start = (bf16[128,4096]{1,0:T(8,128)(2,1)S(1)}, bf16[128,4096]{1,0:T(8,128)(2,1)}, u32[]{:S(2)}) copy-start(bf16[128,4096]{1,0:T(8,128)(2,1)} %gla_query.1) | copy-start | bytes 3145732
  2.5 0.7 copy-start.1
  3.2 0.7 copy-start.2

commit v4 on v3

--- a/solution.py
+++ b/solution.py
@@ -175,8 +175,11 @@
         return 0
 
     lax.fori_loop(0, nb // 2, gained, 0)
-
-    spread(attn_query, attn_query_in.at[rank], 4)
+    @pl.when(lax.axis_index("grp") == 1)
+    def _():
+        spread(attn_query, attn_query_in.at[rank], 4)
+
+
     settle(own_query, local.at[11])
     causal = subs >= lanes
 
@@ -213,6 +216,10 @@
 
     arrive(fade_in.at[0 : n - 1], fade_in.at[0], 0)
     arrive(state_in.at[0 : n - 1], state_in.at[0], 1)
+    @pl.when(lax.axis_index("grp") == 0)
+    def _():
+        spread(attn_query, attn_query_in.at[rank], 4)
+
 
     def scan(i, state):
         for u in range(2):

time: 101 us -> 97.8 us (0.968)
  Pallas kernels: 94.8 us -> 91.1 us
    pallas_call x1, Pallas kernels: 94.8 us -> 91.1 us  [body(): pl.pallas_call(functools.partial(kernel, n), out_shape=(out, out), in_spe...]
where the time goes in v4:
time: 97.8 us; the launch traced here: 97 us
  Pallas kernels  91.1 us (93%)
  local copies, waits for them, and re-layouts  5.25 us (5%)
    pallas_call x1, Pallas kernels, body(): pl.pallas_call(functools.partial(kernel, n), out_shape=(out, out), in_spe...  91.1 us
    unnamed x10, local copies, waits for them, and re-layouts  5.25 us

profile of v4, /device:TPU:16, one launch (start us, length us, event | category | flops | bytes accessed | tf_op | source)
XLA Modules:
  0.0 97.0 jit_solution(14047690048713504998)
XLA Ops:
  0.6 0.0 copy-start.3
  0.6 0.6 copy-done.3
  1.3 0.0 copy-start
  1.3 1.2 %copy-done = bf16[128,4096]{1,0:T(8,128)(2,1)S(1)} copy-done((bf16[128,4096]{1,0:T(8,128)(2,1)S(1)}, bf16[128,4096]{1,0:T(8,128)(2,1)}, u32[]{:S(2)}) %copy-start) | copy-done | bytes 1048600
  2.5 0.0 copy-start.1
  2.5 0.7 copy-done.1
  3.2 0.0 copy-start.2
  3.2 0.7 copy-done.2
  4.0 91.1 %shard_map.95 = (bf16[128,4096]{1,0:T(8,128)(2,1)S(1)}, bf16[128,4096]{1,0:T(8,128)(2,1)S(1)}) custom-call(s32[8]{0:T(128)S(1)} %copy-done.3, f32[32,128]{1,0:T(8,128)S(1)} %bitcast.2, f32[32,128]{1,0:T(8,128)S(1)} %bitcast.3, bf16[128,4096]{1,0:T(8,128)(2,1)S(1)} %copy-done, bf16[128,4096]{1,0:T(8,128)(2,1)} %gla_key.1, bf16[128,4096]{1,0:T(8,128)(2,1)} %gla_value.1, ...), custom_call_target="tpu_custom_call" | custom-call | tf_op jit(solution)/shard_map/pallas_call | solution.py:418
  95.0 1.0 %copy.12 = bf16[128,4096]{1,0:T(8,128)(2,1)} copy(bf16[128,4096]{1,0:T(8,128)(2,1)S(1)} %get-tuple-element.4) | data formatting | bytes 2097152
  96.0 1.0 copy.13
Async XLA Ops:
  0.6 0.7 copy-start.3
  1.3 1.2 %copy-start = (bf16[128,4096]{1,0:T(8,128)(2,1)S(1)}, bf16[128,4096]{1,0:T(8,128)(2,1)}, u32[]{:S(2)}) copy-start(bf16[128,4096]{1,0:T(8,128)(2,1)} %gla_query.1) | copy-start | bytes 3145732
  2.5 0.7 copy-start.1
  3.2 0.7 copy-start.2

commit v5 on v4

--- a/solution.py
+++ b/solution.py
@@ -175,11 +175,6 @@
         return 0
 
     lax.fori_loop(0, nb // 2, gained, 0)
-    @pl.when(lax.axis_index("grp") == 1)
-    def _():
-        spread(attn_query, attn_query_in.at[rank], 4)
-
-
     settle(own_query, local.at[11])
     causal = subs >= lanes
 
@@ -207,6 +202,10 @@
         return 0
 
     lax.fori_loop(0, nb // 2, within, 0)
+    @pl.when(lax.axis_index("grp") == 1)
+    def _():
+        spread(attn_query, attn_query_in.at[rank], 4)
+
     arrive(attn_key_in.at[halo : halo + nb - 1], attn_key_in.at[halo], 2)
 
     @pl.when(half == 0)

time: 97.8 us -> 97.8 us (level)
  no operation moved by 1% of the time
where the time goes in v5:
time: 97.8 us; the launch traced here: 96.4 us
  Pallas kernels  90.5 us (93%)
  local copies, waits for them, and re-layouts  5.25 us (5%)
    pallas_call x1, Pallas kernels, body(): pl.pallas_call(functools.partial(kernel, n), out_shape=(out, out), in_spe...  90.5 us
    unnamed x10, local copies, waits for them, and re-layouts  5.25 us

profile of v5, /device:TPU:16, one launch (start us, length us, event | category | flops | bytes accessed | tf_op | source)
XLA Modules:
  0.0 96.4 jit_solution(13689484334311256481)
XLA Ops:
  0.6 0.0 copy-start.3
  0.6 0.6 copy-done.3
  1.3 0.0 copy-start
  1.3 1.2 %copy-done = bf16[128,4096]{1,0:T(8,128)(2,1)S(1)} copy-done((bf16[128,4096]{1,0:T(8,128)(2,1)S(1)}, bf16[128,4096]{1,0:T(8,128)(2,1)}, u32[]{:S(2)}) %copy-start) | copy-done | bytes 1048600
  2.5 0.0 copy-start.1
  2.5 0.7 copy-done.1
  3.2 0.0 copy-start.2
  3.2 0.7 copy-done.2
  4.0 90.5 %shard_map.95 = (bf16[128,4096]{1,0:T(8,128)(2,1)S(1)}, bf16[128,4096]{1,0:T(8,128)(2,1)S(1)}) custom-call(s32[8]{0:T(128)S(1)} %copy-done.3, f32[32,128]{1,0:T(8,128)S(1)} %bitcast.2, f32[32,128]{1,0:T(8,128)S(1)} %bitcast.3, bf16[128,4096]{1,0:T(8,128)(2,1)S(1)} %copy-done, bf16[128,4096]{1,0:T(8,128)(2,1)} %gla_key.1, bf16[128,4096]{1,0:T(8,128)(2,1)} %gla_value.1, ...), custom_call_target="tpu_custom_call" | custom-call | tf_op jit(solution)/shard_map/pallas_call | solution.py:417
  94.4 1.0 %copy.12 = bf16[128,4096]{1,0:T(8,128)(2,1)} copy(bf16[128,4096]{1,0:T(8,128)(2,1)S(1)} %get-tuple-element.4) | data formatting | bytes 2097152
  95.4 1.0 %copy.13 = bf16[128,4096]{1,0:T(8,128)(2,1)} copy(bf16[128,4096]{1,0:T(8,128)(2,1)S(1)} %get-tuple-element.5) | data formatting | bytes 2097152
Async XLA Ops:
  0.6 0.7 copy-start.3
  1.3 1.2 %copy-start = (bf16[128,4096]{1,0:T(8,128)(2,1)S(1)}, bf16[128,4096]{1,0:T(8,128)(2,1)}, u32[]{:S(2)}) copy-start(bf16[128,4096]{1,0:T(8,128)(2,1)} %gla_query.1) | copy-start | bytes 3145732
  2.5 0.7 copy-start.1
  3.2 0.7 copy-start.2

commit v6 on v5

--- a/solution.py
+++ b/solution.py
@@ -208,10 +208,6 @@
 
     arrive(attn_key_in.at[halo : halo + nb - 1], attn_key_in.at[halo], 2)
 
-    @pl.when(half == 0)
-    def _():
-        push(attn_key_in.at[nb : nb + halo], attn_key_in.at[0:halo], 5, partner)
-
 
     arrive(fade_in.at[0 : n - 1], fade_in.at[0], 0)
     arrive(state_in.at[0 : n - 1], state_in.at[0], 1)
@@ -239,6 +235,11 @@
 
     lax.fori_loop(1, n, enter, 0)
     pltpu.make_async_copy(entering_out.at[place], mine, local.at[3]).start()
+
+    @pl.when(half == 0)
+    def _():
+        push(attn_key_in.at[nb : nb + halo], attn_key_in.at[0:halo], 5, partner)
+
 
     arrive(attn_query_in.at[0 : nb - 1], attn_query_in.at[0], 4)
 

time: 97.8 us -> 97.9 us (level)
  no operation moved by 1% of the time
where the time goes in v6:
time: 97.9 us; the launch traced here: 97.3 us
  Pallas kernels  91.4 us (93%)
  local copies, waits for them, and re-layouts  5.25 us (5%)
    pallas_call x1, Pallas kernels, body(): pl.pallas_call(functools.partial(kernel, n), out_shape=(out, out), in_spe...  91.4 us
    unnamed x10, local copies, waits for them, and re-layouts  5.25 us

profile of v6, /device:TPU:16, one launch (start us, length us, event | category | flops | bytes accessed | tf_op | source)
XLA Modules:
  0.0 97.3 jit_solution(9775596036140971095)
XLA Ops:
  0.6 0.0 copy-start.3
  0.6 0.6 copy-done.3
  1.3 0.0 copy-start
  1.3 1.2 %copy-done = bf16[128,4096]{1,0:T(8,128)(2,1)S(1)} copy-done((bf16[128,4096]{1,0:T(8,128)(2,1)S(1)}, bf16[128,4096]{1,0:T(8,128)(2,1)}, u32[]{:S(2)}) %copy-start) | copy-done | bytes 1048600
  2.5 0.0 copy-start.1
  2.5 0.7 copy-done.1
  3.2 0.0 copy-start.2
  3.2 0.7 copy-done.2
  4.0 91.4 %shard_map.95 = (bf16[128,4096]{1,0:T(8,128)(2,1)S(1)}, bf16[128,4096]{1,0:T(8,128)(2,1)S(1)}) custom-call(s32[8]{0:T(128)S(1)} %copy-done.3, f32[32,128]{1,0:T(8,128)S(1)} %bitcast.2, f32[32,128]{1,0:T(8,128)S(1)} %bitcast.3, bf16[128,4096]{1,0:T(8,128)(2,1)S(1)} %copy-done, bf16[128,4096]{1,0:T(8,128)(2,1)} %gla_key.1, bf16[128,4096]{1,0:T(8,128)(2,1)} %gla_value.1, ...), custom_call_target="tpu_custom_call" | custom-call | tf_op jit(solution)/shard_map/pallas_call | solution.py:418
  95.4 1.0 copy.12
  96.4 1.0 copy.13
Async XLA Ops:
  0.6 0.7 copy-start.3
  1.3 1.2 %copy-start = (bf16[128,4096]{1,0:T(8,128)(2,1)S(1)}, bf16[128,4096]{1,0:T(8,128)(2,1)}, u32[]{:S(2)}) copy-start(bf16[128,4096]{1,0:T(8,128)(2,1)} %gla_query.1) | copy-start | bytes 3145732
  2.5 0.7 copy-start.1
  3.2 0.7 copy-start.2
